TPU v7x, 32 devices: a whole 2x2x4 slice. The times are simulated.
32 devices in a mesh: groups: 2 (over x), vocab: 16 (over z, y, core).
Axes of the slice: x: 2, y: 2, z: 4, core: 2. Of those that a mesh axis runs over, the one named last changes fastest.
Arguments:
- policy_hidden: bfloat16 [128, 6144], P(('groups', 'vocab')), parts along dimension 0, may hold values from -250 to 250
- ref_hidden: bfloat16 [128, 6144], P(('groups', 'vocab')), parts along dimension 0, may hold values from -250 to 250
- policy_head: bfloat16 [6144, 16384], P(None, 'vocab'), may hold values from -0.25 to 0.25
- ref_head: bfloat16 [6144, 16384], P(None, 'vocab'), may hold values from -0.25 to 0.25
- lengths: int32 [2], P('groups'), parts along dimension 0, may hold values from 1 to 128
Outputs:
- kl_token: float32 [128], P(('groups', 'vocab')), parts along dimension 0
- hidden_grad: float32 [128, 6144], P(('groups', 'vocab')), parts along dimension 0
- head_grad: bfloat16 [12288, 16384], P('groups', 'vocab'), parts along dimension 0
There are 2 independent parts, one for each index of `groups`. A program takes and returns all parts, laid end to end along the dimension named above; an argument that names none is the same for every part. Nothing has to cross between parts.
All inputs are finite; a program needn't handle non-finite values.
Results may differ from a plain program's by a relative error of at most 0.0054.
Values may be sent and summed in bfloat16 or wider, within the bound.
A program may use at most 128 MiB of HBM per device.

v0:
```python
import jax
import jax.numpy as jnp
from jax import lax
from jax.sharding import PartitionSpec as P

ROLL = 128


def body(policy_hidden, ref_hidden, policy_head, ref_head, lengths):
    tok_dev = policy_hidden.shape[0]
    tokens = tok_dev * lax.axis_size("vocab")
    stacked = jnp.stack((policy_hidden, ref_hidden))

    def logits_of(piece):
        return jnp.stack(
            (
                jnp.dot(piece[0], policy_head, preferred_element_type=jnp.float32),
                jnp.dot(piece[1], ref_head, preferred_element_type=jnp.float32),
            )
        )

    both = logits_of(lax.all_gather(stacked, "vocab", axis=1, tiled=True))
    policy_logits = both[0]
    ref_logits = both[1]
    policy_top, ref_top = lax.pmax(
        (jnp.max(policy_logits, axis=1), jnp.max(ref_logits, axis=1)), "vocab"
    )
    policy_exp = jnp.exp(policy_logits - policy_top[:, None])
    policy_sum = jnp.sum(policy_exp, axis=1)
    ref_sum = jnp.sum(jnp.exp(ref_logits - ref_top[:, None]), axis=1)
    numerator = jnp.sum(policy_exp * (policy_logits - ref_logits), axis=1)
    policy_sum, ref_sum, numerator = lax.psum((policy_sum, ref_sum, numerator), "vocab")
    policy_lse = policy_top + jnp.log(policy_sum)
    ref_lse = ref_top + jnp.log(ref_sum)
    kl = numerator / policy_sum - policy_lse + ref_lse
    positions = jnp.arange(tokens, dtype=jnp.int32)
    row_count = lengths.shape[0]
    table = (positions // ROLL)[:, None] == jnp.arange(row_count, dtype=jnp.int32)[None, :]
    limits = jnp.sum(jnp.where(table, lengths[None, :], 0), axis=1)
    token_mask = (positions % ROLL < limits).astype(jnp.float32)
    weights = token_mask / jnp.float32(ROLL * row_count)
    own_first = lax.axis_index("vocab") * tok_dev
    kl_token = lax.dynamic_slice_in_dim(token_mask * kl, own_first, tok_dev)
    contract_rows = (((0,), (0,)), ((), ()))
    piece = lax.all_gather(stacked, "vocab", axis=1, tiled=True)
    logits = logits_of(piece)
    policy_logp = logits[0] - policy_lse[:, None]
    ref_logp = logits[1] - ref_lse[:, None]
    prob = jnp.exp(policy_logp)
    kl_rows = kl[:, None]
    weight_rows = weights[:, None]
    grad_piece = (weight_rows * prob * (policy_logp - ref_logp - kl_rows)).astype(jnp.bfloat16)
    head_total = lax.dot_general(
        piece[0], grad_piece, contract_rows, preferred_element_type=jnp.float32
    )
    accumulate_grad_table = grad_piece
    head_total, grad_table = (head_total, accumulate_grad_table)
    contract_vocab = (((1,), (1,)), ((), ()))
    grad_piece = grad_table
    hidden_grad = lax.psum_scatter(
        lax.dot_general(
            grad_piece, policy_head, contract_vocab, preferred_element_type=jnp.float32
        ),
        "vocab",
        scatter_dimension=0,
        tiled=True,
    )
    return (kl_token, hidden_grad, head_total.astype(jnp.bfloat16))


def solution(mesh):
    return jax.shard_map(
        body,
        mesh=mesh,
        in_specs=(
            P(("groups", "vocab"), None),
            P(("groups", "vocab"), None),
            P(None, "vocab"),
            P(None, "vocab"),
            P("groups"),
        ),
        out_specs=(P(("groups", "vocab")), P(("groups", "vocab"), None), P("groups", "vocab")),
        check_vma=False,
    )
```

profile of v0, /device:TPU:0, one launch (start us, length us, event | category | flops | bytes accessed | tf_op | source)
XLA Modules:
  0.0 239.7 jit_solution(16156279201405296855)
XLA Ops:
  7.2 0.0 all-gather.2.cloned.1.call-start
  7.2 0.9 pad_maximum_fusion
  8.1 0.7 copy.8
  8.8 0.0 all-gather.2.cloned.1.call-update
  8.9 0.0 all-reduce.5.cloned.1.call-start
  9.6 1.2 dynamic-slice
  11.5 41.8 %all-gather.2.cloned.1.call-done = bf16[2,64,6144]{2,0,1:T(2,128)(2,1)} async-done(((bf16[2,4,6144]{2,0,1:T(2,128)(2,1)}), bf16[2,64,6144]{2,0,1:T(2,128)(2,1)}) %all-gather.2.cloned.1.call-update) | async-done | bytes 1572880 | tf_op jit(solution)/shard_map/all_gather | solution.py:22
  53.3 4.5 %fusion.4 = (bf16[1,64,6144]{2,0,1:T(2,128)(2,1)S(1)}, bf16[1,64,6144]{2,0,1:T(2,128)(2,1)S(1)}) fusion(bf16[2,64,6144]{2,0,1:T(2,128)(2,1)} %all-gather.2.cloned.1.call-done), kind=kLoop, calls=%fused_computation.23 | loop fusion | bytes 3145728 | tf_op jit(solution)/shard_map/slice | solution.py:18
  57.7 0.0 slice-start.1
  57.7 0.0 slice-start.2
  57.8 7.1 %fusion.5 = (f32[64]{0:T(128)S(1)}, f32[64,1024]{1,0:T(8,128)S(1)}) fusion(bf16[6144,1024]{1,0:T(8,128)(2,1)} %param.8, bf16[1,64,6144]{2,0,1:T(2,128)(2,1)S(1)} %get-tuple-element.15), kind=kOutput, calls=%fused_computation.24 | convolution fusion | flops 805371840 | bytes 13631744 | tf_op jit(solution)/shard_map/dot_general | solution.py:18
  64.9 0.0 slice-done
  64.9 0.0 slice-done.1
  64.9 0.0 slice-done.2
  64.9 2.4 %fusion.6 = (f32[64]{0:T(128)S(1)}, f32[64,1024]{1,0:T(8,128)S(1)}) fusion(bf16[6144,1024]{1,0:T(8,128)(2,1)S(1)} %bitcast.20, bf16[1,64,6144]{2,0,1:T(2,128)(2,1)S(1)} %get-tuple-element.16), kind=kOutput, calls=%fused_computation.25 | convolution fusion | flops 805371840 | bytes 13631744 | tf_op jit(solution)/shard_map/dot_general | solution.py:17
  67.3 31.6 %all-reduce.2 = (f32[64]{0:T(128)S(1)}, f32[64]{0:T(128)S(1)}) all-reduce(f32[64]{0:T(128)S(1)} %get-tuple-element.17, f32[64]{0:T(128)S(1)} %get-tuple-element.19), channel_id=1, replica_groups=mesh['groups'=2,'vocab'=16] {'vocab'}, use_global_device_ids=true, to_apply=%region_7.0 | all-reduce | flops 128 | bytes 1024 | tf_op jit(solution)/shard_map/pmax | solution.py:25
  98.9 0.3 multiply_reduce_fusion
  99.2 29.5 %all-reduce.1 = (f32[64]{0:T(128)S(1)}, f32[64]{0:T(128)S(1)}, f32[64]{0:T(128)S(1)}) all-reduce(f32[64]{0:T(128)S(1)} %get-tuple-element.5, f32[64]{0:T(128)S(1)} %get-tuple-element.4, f32[64]{0:T(128)S(1)} %get-tuple-element.3), channel_id=1, replica_groups=mesh['groups'=2,'vocab'=16] {'vocab'}, use_global_device_ids=true, to_apply=%region_9.0 | all-reduce | flops 192 | bytes 1536 | tf_op jit(solution)/shard_map/psum | solution.py:32
  128.7 9.7 %fusion.7 = f32[64,6144]{1,0:T(8,128)} fusion(bf16[6144,1024]{1,0:T(8,128)(2,1)} %param.7, f32[64,1024]{1,0:T(8,128)S(1)} %get-tuple-element.18, f32[64,1024]{1,0:T(8,128)S(1)} %get-tuple-element.20, f32[64]{0:T(128)S(1)} %get-tuple-element.12, f32[64]{0:T(128)S(1)} %get-tuple-element.14, f32[64]{0:T(128)S(1)} %get-tuple-element.13, ...), kind=kOutput, calls=%fused_computation.26 | convolution fusion | flops 805765120 | bytes 14681088 | tf_op jit(solution)/shard_map/dot_general | solution.py:61
  138.4 0.0 all-reduce.5.cloned.1.call-update
  138.4 0.6 dynamic_slice.3
  139.0 6.7 %convolution_convert_fusion = bf16[6144,1024]{1,0:T(8,128)(2,1)} fusion(bf16[1,64,6144]{2,0,1:T(2,128)(2,1)S(1)} %get-tuple-element.16, f32[64,1024]{1,0:T(8,128)S(1)} %get-tuple-element.18, f32[64,1024]{1,0:T(8,128)S(1)} %get-tuple-element.20, f32[64]{0:T(128)S(1)} %get-tuple-element.12, f32[64]{0:T(128)S(1)} %get-tuple-element.14, ...), kind=kOutput, calls=%fused_computation | convolution fusion | flops 812056576 | bytes 13894656 | tf_op jit(solution)/shard_map/dot_general | solution.py:53
  145.7 85.5 %all-reduce.5.cloned.1.call-done = f32[64,6144]{1,0:T(8,128)} async-done(((f32[64,6144]{1,0:T(8,128)}), f32[64,6144]{1,0:T(8,128)}) %all-reduce.5.cloned.1.call-update) | async-done | bytes 1572880
  231.3 1.6 constant_dynamic-slice_fusion
  (3 shorter events, 0.0 us)
Async XLA Ops:
  7.2 46.1 %all-gather.2.cloned.1.call-start = ((), (), s32[]{:S(2)}) async-start(), calls=%async_computation | async-start | bytes 1671168 | tf_op jit(solution)/shard_map/all_gather | solution.py:22
  8.9 222.4 %all-reduce.5.cloned.1.call-start = ((), (), s32[]{:S(2)}) async-start(), calls=%async_computation.1 | async-start | bytes 3145728
  53.3 11.6 %slice-start = ((s8[12582912]{0:T(1024)(128)(4,1)}), s8[4194304]{0:T(1024)(128)(4,1)S(1)}, s32[]{:S(2)}) async-start(s8[12582912]{0:T(1024)(128)(4,1)} %bitcast.19), calls=%async_computation.2 | async-start | bytes 8388608
  57.7 7.2 %slice-start.1 = ((s8[12582912]{0:T(1024)(128)(4,1)}), s8[4194304]{0:T(1024)(128)(4,1)S(1)}, s32[]{:S(2)}) async-start(s8[12582912]{0:T(1024)(128)(4,1)} %bitcast.19), calls=%async_computation.3 | async-start | bytes 8388608
  57.7 7.2 %slice-start.2 = ((s8[12582912]{0:T(1024)(128)(4,1)}), s8[4194304]{0:T(1024)(128)(4,1)S(1)}, s32[]{:S(2)}) async-start(s8[12582912]{0:T(1024)(128)(4,1)} %bitcast.19), calls=%async_computation.4 | async-start | bytes 8388608
Sparse Core Ops, SparseCore 0:
  10.9 42.3 all-gather.1
  138.5 92.6 all-reduce.4
where the time goes:
time: 240 us
  waiting for transfers between devices  127 us (53%)
  blocking collectives  61.1 us (25%)
  matrix products  26 us (11%)
  between operations  15.4 us (6%)
  local copies, waits for them, and re-layouts  8.63 us (4%)
    unnamed x3, waiting for transfers between devices  85.6 us
    all_gather x1, waiting for transfers between devices, body(): both = logits_of(lax.all_gather(stacked, 'vocab', axis=1, tiled=True))  41.8 us
    pmax x1, blocking collectives, body(): lax.pmax((jnp.max(policy_logits, axis=1), jnp.max(ref_logits, axis=1)), '...  31.6 us
    psum x1, blocking collectives, body(): lax.psum((policy_sum, ref_sum, numerator), 'vocab')  29.5 us
    dot_general x1, matrix products, body(): lax.dot_general(grad_piece, policy_head, contract_vocab, preferred_elemen...  9.71 us
    dot_general x1, matrix products, logits_of(): jnp.dot(piece[1], ref_head, preferred_element_type=jnp.float32)  7.12 us
    dot_general x1, matrix products, body(): lax.dot_general(piece[0], grad_piece, contract_rows, preferred_element_ty...  6.7 us
  transfers between devices with their start and end apart: 2, of which 2 were waited for; matrix products, arithmetic and copies ran while one was open for 4% of the time, Pallas kernels for 0%

commit v1 on v0

--- a/solution.py
+++ b/solution.py
@@ -19,17 +19,29 @@
             )
         )
 
-    both = logits_of(lax.all_gather(stacked, "vocab", axis=1, tiled=True))
+    piece = lax.all_gather(stacked, "vocab", axis=1, tiled=True)
+    both = logits_of(piece)
     policy_logits = both[0]
     ref_logits = both[1]
-    policy_top, ref_top = lax.pmax(
-        (jnp.max(policy_logits, axis=1), jnp.max(ref_logits, axis=1)), "vocab"
+    own_top = jnp.max(policy_logits, axis=1)
+    own_ref_top = jnp.max(ref_logits, axis=1)
+    policy_exp = jnp.exp(policy_logits - own_top[:, None])
+    stats = jnp.stack(
+        (
+            own_top,
+            own_ref_top,
+            jnp.sum(policy_exp, axis=1),
+            jnp.sum(jnp.exp(ref_logits - own_ref_top[:, None]), axis=1),
+            jnp.sum(policy_exp * (policy_logits - ref_logits), axis=1),
+        )
     )
-    policy_exp = jnp.exp(policy_logits - policy_top[:, None])
-    policy_sum = jnp.sum(policy_exp, axis=1)
-    ref_sum = jnp.sum(jnp.exp(ref_logits - ref_top[:, None]), axis=1)
-    numerator = jnp.sum(policy_exp * (policy_logits - ref_logits), axis=1)
-    policy_sum, ref_sum, numerator = lax.psum((policy_sum, ref_sum, numerator), "vocab")
+    stats = lax.all_gather(stats, "vocab", axis=0)
+    policy_top = jnp.max(stats[:, 0], axis=0)
+    ref_top = jnp.max(stats[:, 1], axis=0)
+    policy_scale = jnp.exp(stats[:, 0] - policy_top)
+    policy_sum = jnp.sum(stats[:, 2] * policy_scale, axis=0)
+    ref_sum = jnp.sum(stats[:, 3] * jnp.exp(stats[:, 1] - ref_top), axis=0)
+    numerator = jnp.sum(stats[:, 4] * policy_scale, axis=0)
     policy_lse = policy_top + jnp.log(policy_sum)
     ref_lse = ref_top + jnp.log(ref_sum)
     kl = numerator / policy_sum - policy_lse + ref_lse
@@ -42,8 +54,7 @@
     own_first = lax.axis_index("vocab") * tok_dev
     kl_token = lax.dynamic_slice_in_dim(token_mask * kl, own_first, tok_dev)
     contract_rows = (((0,), (0,)), ((), ()))
-    piece = lax.all_gather(stacked, "vocab", axis=1, tiled=True)
-    logits = logits_of(piece)
+    logits = both
     policy_logp = logits[0] - policy_lse[:, None]
     ref_logp = logits[1] - ref_lse[:, None]
     prob = jnp.exp(policy_logp)

time: 240 us -> 199 us (0.83)
  blocking collectives: 61.1 us -> 19.5 us
    pmax x1 -> x0, blocking collectives: 31.6 us -> none  [body(): lax.pmax((jnp.max(policy_logits, axis=1), jnp.max(ref_logits, axis=1)), '...]
    psum x1 -> x0, blocking collectives: 29.5 us -> none  [body(): lax.psum((policy_sum, ref_sum, numerator), 'vocab')]
    all_gather x0 -> x1, blocking collectives: none -> 19.5 us  [body(): stats = lax.all_gather(stats, 'vocab', axis=0)]
where the time goes in v1:
time: 199 us; the launch traced here: 198 us
  waiting for transfers between devices  127 us (64%)
  matrix products  26 us (13%)
  blocking collectives  19.5 us (10%)
  between operations  15.4 us (8%)
  local copies, waits for them, and re-layouts  8.66 us (4%)
    unnamed x3, waiting for transfers between devices  85.6 us
    all_gather x1, waiting for transfers between devices, body(): piece = lax.all_gather(stacked, 'vocab', axis=1, tiled=True)  41.8 us
    all_gather x1, blocking collectives, body(): stats = lax.all_gather(stats, 'vocab', axis=0)  19.5 us
    dot_general x1, matrix products, body(): lax.dot_general(grad_piece, policy_head, contract_vocab, preferred_elemen...  9.72 us
    dot_general x1, matrix products, logits_of(): jnp.dot(piece[1], ref_head, preferred_element_type=jnp.float32)  7.12 us
    dot_general x1, matrix products, body(): lax.dot_general(piece[0], grad_piece, contract_rows, preferred_element_ty...  6.7 us
    slice x1, local copies, waits for them, and re-layouts, logits_of(): piece[1]  4.45 us
  transfers between devices with their start and end apart: 2, of which 2 were waited for; matrix products, arithmetic and copies ran while one was open for 4% of the time, Pallas kernels for 0%

profile of v1, /device:TPU:0, one launch (start us, length us, event | category | flops | bytes accessed | tf_op | source)
XLA Modules:
  0.0 198.3 jit_solution(6482537483555158075)
XLA Ops:
  7.2 0.0 all-gather.4.cloned.1.call-start
  7.2 0.9 pad_maximum_fusion
  8.1 0.7 copy.14
  8.8 0.0 all-gather.4.cloned.1.call-update
  8.9 0.0 all-reduce.3.cloned.1.call-start
  9.6 1.2 dynamic-slice
  11.5 41.8 %all-gather.4.cloned.1.call-done = bf16[2,64,6144]{2,0,1:T(2,128)(2,1)} async-done(((bf16[2,4,6144]{2,0,1:T(2,128)(2,1)}), bf16[2,64,6144]{2,0,1:T(2,128)(2,1)}) %all-gather.4.cloned.1.call-update) | async-done | bytes 1572880 | tf_op jit(solution)/shard_map/all_gather | solution.py:22
  53.3 0.0 slice-start
  53.3 4.5 %fusion.4 = (bf16[1,64,6144]{2,0,1:T(2,128)(2,1)S(1)}, bf16[1,64,6144]{2,0,1:T(2,128)(2,1)S(1)}) fusion(bf16[2,64,6144]{2,0,1:T(2,128)(2,1)} %all-gather.4.cloned.1.call-done), kind=kLoop, calls=%fused_computation.28 | loop fusion | bytes 3145728 | tf_op jit(solution)/shard_map/slice | solution.py:18
  57.7 0.0 slice-start.1
  57.7 0.0 slice-start.2
  57.8 7.1 %fusion.7 = (f32[64]{0:T(128)S(1)}, f32[64,1024]{1,0:T(8,128)S(1)}) fusion(bf16[6144,1024]{1,0:T(8,128)(2,1)} %param.8, bf16[1,64,6144]{2,0,1:T(2,128)(2,1)S(1)} %get-tuple-element.12), kind=kOutput, calls=%fused_computation.31 | convolution fusion | flops 805371840 | bytes 13631744 | tf_op jit(solution)/shard_map/dot_general | solution.py:18
  64.9 0.0 slice-done
  64.9 0.0 slice-done.1
  64.9 0.0 slice-done.2
  64.9 2.4 %fusion.6 = (f32[64]{0:T(128)S(1)}, f32[64,1024]{1,0:T(8,128)S(1)}) fusion(bf16[6144,1024]{1,0:T(8,128)(2,1)S(1)} %bitcast.37, bf16[1,64,6144]{2,0,1:T(2,128)(2,1)S(1)} %get-tuple-element.13), kind=kOutput, calls=%fused_computation.30 | convolution fusion | flops 805371840 | bytes 13631744 | tf_op jit(solution)/shard_map/dot_general | solution.py:17
  67.3 0.3 multiply_reduce_fusion
  67.6 19.5 %all-gather.1 = f32[16,5,64]{2,1,0:T(8,128)S(1)} all-gather(f32[1,5,64]{2,1,0:T(8,128)S(1)} %bitcast.46), channel_id=2, replica_groups=mesh['groups'=2,'vocab'=16] {'vocab'}, dimensions={0}, use_global_device_ids=true | all-gather | bytes 21760 | tf_op jit(solution)/shard_map/all_gather | solution.py:38
  87.3 9.7 %fusion.8 = f32[64,6144]{1,0:T(8,128)} fusion(bf16[6144,1024]{1,0:T(8,128)(2,1)} %param.7, f32[64,1024]{1,0:T(8,128)S(1)} %get-tuple-element.23, f32[64,1024]{1,0:T(8,128)S(1)} %get-tuple-element.21, f32[64]{0:T(128)S(1)} %get-tuple-element.9, f32[64]{0:T(128)S(1)} %get-tuple-element.11, f32[64]{0:T(128)S(1)} %get-tuple-element.10, f32[64]{0:T(128)S(1)} %get-tuple-element.24), kind=kOutput, calls=%fused_computation.32 | convolution fusion | flops 805765120 | bytes 14681088 | tf_op jit(solution)/shard_map/dot_general | solution.py:72
  97.0 0.0 all-reduce.3.cloned.1.call-update
  97.0 0.6 dynamic_slice.3
  97.6 6.7 %convolution_convert_fusion = bf16[6144,1024]{1,0:T(8,128)(2,1)} fusion(bf16[1,64,6144]{2,0,1:T(2,128)(2,1)S(1)} %get-tuple-element.13, f32[64,1024]{1,0:T(8,128)S(1)} %get-tuple-element.23, f32[64,1024]{1,0:T(8,128)S(1)} %get-tuple-element.21, f32[64]{0:T(128)S(1)} %get-tuple-element.9, f32[64]{0:T(128)S(1)} %get-tuple-element.11, ...), kind=kOutput, calls=%fused_computation | convolution fusion | flops 812056576 | bytes 13894656 | tf_op jit(solution)/shard_map/dot_general | solution.py:64
  104.3 85.6 %all-reduce.3.cloned.1.call-done = f32[64,6144]{1,0:T(8,128)} async-done(((f32[64,6144]{1,0:T(8,128)}), f32[64,6144]{1,0:T(8,128)}) %all-reduce.3.cloned.1.call-update) | async-done | bytes 1572880
  189.9 1.6 constant_dynamic-slice_fusion
  (7 shorter events, 0.2 us)
Async XLA Ops:
  7.2 46.1 %all-gather.4.cloned.1.call-start = ((), (), s32[]{:S(2)}) async-start(), calls=%async_computation | async-start | bytes 1671168 | tf_op jit(solution)/shard_map/all_gather | solution.py:22
  8.9 181.0 %all-reduce.3.cloned.1.call-start = ((), (), s32[]{:S(2)}) async-start(), calls=%async_computation.1 | async-start | bytes 3145728
  53.3 11.6 %slice-start = ((s8[12582912]{0:T(1024)(128)(4,1)}), s8[4194304]{0:T(1024)(128)(4,1)S(1)}, s32[]{:S(2)}) async-start(s8[12582912]{0:T(1024)(128)(4,1)} %bitcast.36), calls=%async_computation.2 | async-start | bytes 8388608
  57.7 7.2 %slice-start.1 = ((s8[12582912]{0:T(1024)(128)(4,1)}), s8[4194304]{0:T(1024)(128)(4,1)S(1)}, s32[]{:S(2)}) async-start(s8[12582912]{0:T(1024)(128)(4,1)} %bitcast.36), calls=%async_computation.3 | async-start | bytes 8388608
  57.7 7.2 %slice-start.2 = ((s8[12582912]{0:T(1024)(128)(4,1)}), s8[4194304]{0:T(1024)(128)(4,1)S(1)}, s32[]{:S(2)}) async-start(s8[12582912]{0:T(1024)(128)(4,1)} %bitcast.36), calls=%async_computation.4 | async-start | bytes 8388608
Sparse Core Ops, SparseCore 0:
  10.9 42.3 all-gather.3
  97.1 92.7 all-reduce.2

commit v2 on v0

v2 whole, which is shorter than its diff:
```python
import functools

import jax
import jax.numpy as jnp
from jax import lax
from jax.experimental import pallas as pl
from jax.experimental.pallas import tpu as pltpu
from jax.sharding import PartitionSpec as P

ROLL = 128
TILE = 256
MESH = pl.DeviceIdType.MESH
F32 = jnp.float32
BF16 = jnp.bfloat16


def kernel(
    n,
    units,
    lengths,
    policy_head,
    ref_head,
    kl_out,
    hidden_out,
    grad_out,
    rows_out,
    gathered,
    ref_rows,
    policy_w,
    ref_w,
    policy_logits,
    ref_logits,
    stats,
    total,
    outgoing,
    sibling_in,
    ring_out,
    ring_in,
    head_sem,
    gather_send,
    gather_recv,
    stats_send,
    stats_recv,
    pair_send,
    pair_recv,
    ring_send,
    ring_recv,
):
    depth, columns = policy_w.shape
    half = depth // 2
    quarter = depth // 4
    eighth = depth // 8
    tokens = rows_out.shape[0]
    padded = stats.shape[2]
    chips = n // 2
    me = lax.axis_index("vocab")
    core = me % 2
    chip = me // 2
    snake = chips == 8

    def position_of(k):
        if not snake:
            return k
        z, y = k // 2, k % 2
        return (1 - y) * z + y * (chips - 1 - z)

    def chip_at(p):
        p = (p + chips) % chips
        if not snake:
            return p
        far = p // (chips // 2)
        return (1 - far) * 2 * p + far * (2 * (chips - 1 - p) + 1)

    pos = position_of(chip)
    right = chip_at(pos + 1) * 2 + core
    left = chip_at(pos - 1) * 2 + core
    sibling = chip * 2 + 1 - core

    longer, shorter = chips // 2, chips - 1 - chips // 2
    limits = ((longer, shorter), (shorter, longer))

    head_copies = []
    for j in range(2):
        span = pl.ds(j * half, half)
        for which, (hbm, vmem) in enumerate(((policy_head, policy_w), (ref_head, ref_w))):
            copy = pltpu.make_async_copy(hbm.at[span], vmem.at[span], head_sem.at[j, which])
            copy.start()
            head_copies.append(copy)

    barrier = pltpu.get_barrier_semaphore()

    def greet(i, carry):
        pl.semaphore_signal(
            barrier, inc=1, device_id={"vocab": (me + i) % n}, device_id_type=MESH
        )
        return carry

    lax.fori_loop(1, n, greet, 0)
    pl.semaphore_wait(barrier, n - 1)

    sent = []

    def remote(src, dst, send, recv, device):
        return pltpu.make_async_remote_copy(
            src_ref=src,
            dst_ref=dst,
            send_sem=send,
            recv_sem=recv,
            device_id={"vocab": device},
            device_id_type=MESH,
        )

    def send(src, dst, send_sem, recv_sem, device):
        copy = remote(src, dst, send_sem, recv_sem, device)
        copy.start()
        sent.append(copy)

    def pass_on(j, src, owner, lane, step, device):
        send(
            src,
            gathered.at[j, owner],
            gather_send.at[j, lane, step],
            gather_recv.at[j, owner],
            device,
        )

    def arrived(j, owner):
        slot = gathered.at[j, owner]
        remote(slot, slot, gather_send.at[j, 0, 0], gather_recv.at[j, owner], sibling).wait_recv()

    for j in range(2):
        pass_on(j, units.at[j], me, 0, 0, right)
        pass_on(j, units.at[j], me, 1, 0, left)
        pass_on(j, units.at[j], me, 2, 0, sibling)
    for j in range(2):
        gathered[j, me] = units[j]
    for step in range(1, longer + 1):
        for j in range(2):
            for way in range(2):
                limit = limits[way][j]
                if step > limit:
                    continue
                owner = chip_at(pos - step if way == 0 else pos + step) * 2 + core
                arrived(j, owner)
                if step < limit:
                    pass_on(j, gathered.at[j, owner], owner, way, step, (right, left)[way])
                lane = 2 + way
                pass_on(j, gathered.at[j, owner], owner, lane, step, sibling)

    low = lax.broadcasted_iota(jnp.int32, (8, quarter), 0) < 4
    for j in range(2):
        for k in range(chips):
            arrived(j, k * 2 + 1 - core)
        for group in range(n // 4):
            block = gathered[j, 4 * group : 4 * group + 4].astype(F32)
            for q in range(2):
                part = block[:, 8 * q : 8 * q + 8]
                policy, ref = [], []
                for i in range(2):
                    even, odd = part[2 * i], part[2 * i + 1]
                    policy.append(jnp.where(low, even, pltpu.roll(odd, 4, 0)))
                    ref.append(jnp.where(low, pltpu.roll(even, 4, 0), odd))
                span = pl.ds(j * half + q * quarter, quarter)
                rows = pl.ds(16 * group, 16)
                rows_out[rows, span] = jnp.concatenate(policy, axis=0).astype(BF16)
                ref_rows[rows, span] = jnp.concatenate(ref, axis=0).astype(BF16)
        head_copies[2 * j].wait()
        head_copies[2 * j + 1].wait()
        span = pl.ds(j * half, half)

        @pl.loop(0, columns // TILE)
        def _(i, j=j, span=span):
            cols = pl.ds(pl.multiple_of(i * TILE, TILE), TILE)
            for x, w, out in (
                (rows_out, policy_w, policy_logits),
                (ref_rows, ref_w, ref_logits),
            ):
                product = jnp.dot(x[:, span], w[span, cols], preferred_element_type=F32)
                out[:, cols] = product if j == 0 else out[:, cols] + product

    p, r = policy_logits[...], ref_logits[...]
    p_top = jnp.max(p, axis=1, keepdims=True)
    r_top = jnp.max(r, axis=1, keepdims=True)
    p_exp = jnp.exp(p - p_top)
    p_sum = jnp.sum(p_exp, axis=1, keepdims=True)
    r_sum = jnp.sum(jnp.exp(r - r_top), axis=1, keepdims=True)
    numerator = jnp.sum(p_exp * (p - r), axis=1, keepdims=True)
    lane = lax.broadcasted_iota(jnp.int32, (tokens, 128), 1)
    table = jnp.zeros((tokens, 128), F32)
    for i, column in ((0, p_top), (1, r_top), (2, p_top), (4, p_sum), (5, r_sum), (6, numerator)):
        table = jnp.where(lane == i, column, table)
    if padded > tokens:
        table = jnp.concatenate([table, jnp.ones((padded - tokens, 128), F32)], axis=0)
    stats[me] = table.T[:8]

    def stats_copy(i):
        target = (me + i) % n
        return remote(
            stats.at[me], stats.at[me], stats_send.at[i], stats_recv.at[me], target
        )

    def spread(i, carry):
        stats_copy(i).start()
        return carry

    def collect(i, carry):
        source = (me + n - i) % n
        slot = stats.at[source]
        remote(slot, slot, stats_send.at[i], stats_recv.at[source], source).wait_recv()
        stats_copy(i).wait_send()
        return carry

    lax.fori_loop(1, n, spread, 0)
    lax.fori_loop(1, n, collect, 0)

    top = stats[0]
    for d in range(1, n):
        top = jnp.maximum(top, stats[d])
    sums = jnp.zeros_like(top)
    for d in range(n):
        one = stats[d]
        sums = sums + pltpu.roll(jnp.exp(one - top), 4, 0) * one
    p_lse = top[0:1] + jnp.log(sums[4:5])
    r_lse = top[1:2] + jnp.log(sums[5:6])
    kl = sums[6:7] / sums[4:5] - p_lse + r_lse
    token = lax.broadcasted_iota(jnp.int32, (1, padded), 1)
    row = token // ROLL
    row_count = lengths.shape[0]
    limit = jnp.zeros((1, padded), jnp.int32)
    for i in range(row_count):
        limit = jnp.where(row == i, lengths[i], limit)
    mask = (token - row * ROLL < limit).astype(F32)
    weight = mask / jnp.float32(ROLL * row_count)
    kl_out[...] = mask * kl
    line = lax.broadcasted_iota(jnp.int32, (128, padded), 0)
    table = jnp.where(line == 0, p_lse, jnp.where(line == 1, r_lse, jnp.where(line == 2, kl, weight)))
    table = table.T[:tokens]
    p_lse, r_lse, kl, weight = (table[:, i : i + 1] for i in range(4))

    p_logp = policy_logits[...] - p_lse
    r_logp = ref_logits[...] - r_lse
    grad_out[...] = (weight * jnp.exp(p_logp) * ((p_logp - r_logp) - kl)).astype(BF16)

    low = lax.broadcasted_iota(jnp.int32, (chips, 8, TILE), 1) < 4
    for j in range(2):

        @pl.loop(0, eighth // TILE)
        def _(i, j=j):
            cols = pl.ds(pl.multiple_of(i * TILE, TILE), TILE)
            outs = []
            for a in range(4):
                start = pl.multiple_of(j * half + a * eighth + i * TILE, TILE)
                outs.append(
                    lax.dot_general(
                        grad_out[...],
                        policy_w[pl.ds(start, TILE), :],
                        (((1,), (1,)), ((), ())),
                        preferred_element_type=F32,
                    ).reshape(chips, 8, TILE)
                )
            for c in range(2):
                halves = []
                for a in (0, 2):
                    first, second = outs[a], outs[a + 1]
                    if c == 0:
                        second = pltpu.roll(second, 4, 1)
                    else:
                        first = pltpu.roll(first, 4, 1)
                    halves.append(jnp.where(low, first, second))
                both = jnp.concatenate(halves, axis=1)
                total[j, c, :, :, cols] = both
                outgoing[j, c, :, :, cols] = both.astype(BF16)

        send(
            outgoing.at[j, 1 - core],
            sibling_in.at[j],
            pair_send.at[j],
            pair_recv.at[j],
            sibling,
        )

    def own(j, k):
        return total[j, core, k] + sibling_in[j, k].astype(F32)

    def ring_wait(j, way, step):
        slot = ring_in.at[j, way, step]
        remote(
            slot, slot, ring_send.at[j, way, step], ring_recv.at[j, way, step], sibling
        ).wait_recv()

    for step in range(longer):
        for j in range(2):
            if step == 0:
                remote(
                    sibling_in.at[j], sibling_in.at[j], pair_send.at[j], pair_recv.at[j], sibling
                ).wait_recv()
            for way in range(2):
                limit = limits[way][j]
                if step >= limit:
                    continue
                hops = limit - step
                value = own(j, chip_at(pos + hops if way == 0 else pos - hops))
                if step > 0:
                    ring_wait(j, way, step - 1)
                    value = value + ring_in[j, way, step - 1].astype(F32)
                ring_out[j, way, step] = value.astype(BF16)
                send(
                    ring_out.at[j, way, step],
                    ring_in.at[j, way, step],
                    ring_send.at[j, way, step],
                    ring_recv.at[j, way, step],
                    (right, left)[way],
                )
    for j in range(2):
        value = own(j, chip)
        for way in range(2):
            last = limits[way][j] - 1
            ring_wait(j, way, last)
            value = value + ring_in[j, way, last].astype(F32)
        hidden_out[j] = value
    for copy in sent:
        copy.wait_send()


def body(policy_hidden, ref_hidden, policy_head, ref_head, lengths):
    n = lax.axis_size("vocab")
    tok_dev, depth = policy_hidden.shape
    columns = policy_head.shape[1]
    tokens = tok_dev * n
    chips = n // 2
    padded = -(-tokens // 128) * 128
    steps = chips // 2 + 1
    quarter, eighth = depth // 4, depth // 8
    units = jnp.concatenate((policy_hidden, ref_hidden), axis=0)
    units = units.reshape(8, 2, 2, quarter).transpose(1, 2, 0, 3).reshape(2, 16, quarter)
    vmem = pl.BlockSpec(memory_space=pltpu.VMEM)
    hbm = pl.BlockSpec(memory_space=pl.ANY)
    dma = pltpu.SemaphoreType.DMA
    kl, hidden, grad, rows = pl.pallas_call(
        functools.partial(kernel, n),
        out_shape=(
            jax.ShapeDtypeStruct((1, padded), F32),
            jax.ShapeDtypeStruct((2, 16, eighth), F32),
            jax.ShapeDtypeStruct((tokens, columns), BF16),
            jax.ShapeDtypeStruct((tokens, depth), BF16),
        ),
        in_specs=[vmem, pl.BlockSpec(memory_space=pltpu.SMEM), hbm, hbm],
        out_specs=(vmem,) * 4,
        scratch_shapes=[
            pltpu.VMEM((2, n, 16, quarter), BF16),
            pltpu.VMEM((tokens, depth), BF16),
            pltpu.VMEM((depth, columns), BF16),
            pltpu.VMEM((depth, columns), BF16),
            pltpu.VMEM((tokens, columns), F32),
            pltpu.VMEM((tokens, columns), F32),
            pltpu.VMEM((n, 8, padded), F32),
            pltpu.VMEM((2, 2, chips, 16, eighth), F32),
            pltpu.VMEM((2, 2, chips, 16, eighth), BF16),
            pltpu.VMEM((2, chips, 16, eighth), BF16),
            pltpu.VMEM((2, 2, steps, 16, eighth), BF16),
            pltpu.VMEM((2, 2, steps, 16, eighth), BF16),
            dma((2, 2)),
            dma((2, 4, steps)),
            dma((2, n)),
            dma((n,)),
            dma((n,)),
            dma((2,)),
            dma((2,)),
            dma((2, 2, steps)),
            dma((2, 2, steps)),
        ],
        compiler_params=pltpu.CompilerParams(
            collective_id=0, has_side_effects=True, vmem_limit_bytes=56 * 2**20
        ),
    )(units, lengths, policy_head, ref_head)
    own_first = lax.axis_index("vocab") * tok_dev
    kl_token = lax.dynamic_slice_in_dim(kl[0], own_first, tok_dev)
    hidden_grad = (
        hidden.reshape(2, 4, tok_dev, eighth).transpose(2, 0, 1, 3).reshape(tok_dev, depth)
    )
    head_grad = lax.dot_general(
        rows, grad, (((0,), (0,)), ((), ())), preferred_element_type=F32
    ).astype(BF16)
    return kl_token, hidden_grad, head_grad


def solution(mesh):
    return jax.shard_map(
        body,
        mesh=mesh,
        in_specs=(
            P(("groups", "vocab"), None),
            P(("groups", "vocab"), None),
            P(None, "vocab"),
            P(None, "vocab"),
            P("groups"),
        ),
        out_specs=(P(("groups", "vocab")), P(("groups", "vocab"), None), P("groups", "vocab")),
        check_vma=False,
    )
```

time: 240 us -> 67.3 us (0.28)
  waiting for transfers between devices: 127 us -> 0 us
  blocking collectives: 61.1 us -> 0 us
  Pallas kernels: 0 us -> 52 us
  matrix products: 26 us -> 9.39 us
  between operations: 15.4 us -> 1.29 us
  local copies, waits for them, and re-layouts: 8.63 us -> 2.82 us
    unnamed x3 -> x0, waiting for transfers between devices: 85.6 us -> none
    pallas_call x0 -> x1, Pallas kernels: none -> 52 us  [body(): pl.pallas_call(functools.partial(kernel, n), out_shape=(jax.ShapeDtypeStr...]
    all_gather x1 -> x0, waiting for transfers between devices: 41.8 us -> none  [body(): both = logits_of(lax.all_gather(stacked, 'vocab', axis=1, tiled=True))]
    pmax x1 -> x0, blocking collectives: 31.6 us -> none  [body(): lax.pmax((jnp.max(policy_logits, axis=1), jnp.max(ref_logits, axis=1)), '...]
    psum x1 -> x0, blocking collectives: 29.5 us -> none  [body(): lax.psum((policy_sum, ref_sum, numerator), 'vocab')]
    dot_general x4 -> x1, matrix products: 26 us -> 9.39 us  [body(): lax.dot_general(rows, grad, (((0,), (0,)), ((), ())), preferred_element_t...]
    slice x1 -> x0, local copies, waits for them, and re-layouts: 4.45 us -> none  [logits_of(): piece[1]]
    unnamed x8 -> x0, local copies, waits for them, and re-layouts: 2.84 us -> none
  transfers between devices with their start and end apart: 2 -> 0, of which waited for: 2 -> 0; matrix products, arithmetic and copies ran while one was open for 4% -> 0% of each run, Pallas kernels for 0% -> 0%
where the time goes in v2:
time: 67.3 us; the launch traced here: 67 us
  Pallas kernels  52 us (77%)
  matrix products  9.39 us (14%)
  local copies, waits for them, and re-layouts  2.82 us (4%)
  other arithmetic  1.52 us (2%)
  between operations  1.29 us (2%)
    pallas_call x1, Pallas kernels, body(): pl.pallas_call(functools.partial(kernel, n), out_shape=(jax.ShapeDtypeStr...  52 us
    dot_general x1, matrix products, body(): lax.dot_general(rows, grad, (((0,), (0,)), ((), ())), preferred_element_t...  9.39 us
    reshape x1, local copies, waits for them, and re-layouts, body(): hidden.reshape(2, 4, tok_dev, eighth).transpose(2, 0, 1, 3)  1.56 us
    concatenate x1, other arithmetic, body(): units = jnp.concatenate((policy_hidden, ref_hidden), axis=0)  1.52 us

profile of v2, /device:TPU:0, one launch (start us, length us, event | category | flops | bytes accessed | tf_op | source)
XLA Modules:
  0.0 67.0 jit_solution(17946610303915235261)
XLA Ops:
  1.3 1.5 %pad_maximum_fusion = bf16[8,6144]{1,0:T(8,128)(2,1)} fusion(bf16[4,6144]{1,0:T(4,128)(2,1)} %param.6, bf16[4,6144]{1,0:T(4,128)(2,1)} %param.5), kind=kLoop, calls=%fused_computation.1 | loop fusion | flops 196608 | bytes 196608 | tf_op jit(solution)/shard_map/concatenate | solution.py:334
  2.8 52.0 %shard_map.76 = (f32[1,128]{1,0:T(1,128)}, f32[2,16,768]{2,1,0:T(8,128)}, bf16[64,1024]{1,0:T(8,128)(2,1)}, bf16[64,6144]{1,0:T(8,128)(2,1)}) custom-call(bf16[2,16,1536]{2,1,0:T(8,128)(2,1)} %bitcast.12, s32[1]{0:T(128)S(6)} %copy.9.lengths, bf16[6144,1024]{1,0:T(8,128)(2,1)} %policy_head.1, bf16[6144,1024]{1,0:T(8,128)(2,1)} %ref_head.1), custom_call_target="tpu_custom_call" | custom-call | tf_op jit(solution)/shard_map/pallas_call | solution.py:339
  54.8 1.3 %dynamic-slice_bitcast_fusion = f32[4]{0:T(128)} fusion(f32[1,128]{1,0:T(1,128)} %get-tuple-element.7, s32[]{:T(128)S(6)} %select_n.3), kind=kLoop, calls=%fused_computation.2 | loop fusion | bytes 36 | tf_op jit(solution)/shard_map/dynamic_slice | solution.py:377
  56.0 1.6 %reshape.21 = f32[2,4,4,768]{3,2,1,0:T(4,128)} reshape(f32[2,16,768]{2,1,0:T(8,128)} %get-tuple-element.8) | data formatting | bytes 196608 | tf_op jit(solution)/shard_map/reshape | solution.py:379
  57.6 9.4 %convolution_convert_fusion = bf16[6144,1024]{1,0:T(8,128)(2,1)} fusion(bf16[64,6144]{1,0:T(8,128)(2,1)} %get-tuple-element.9, bf16[64,1024]{1,0:T(8,128)(2,1)} %get-tuple-element.10), kind=kOutput, calls=%fused_computation | convolution fusion | flops 811597824 | bytes 13500416 | tf_op jit(solution)/shard_map/dot_general | solution.py:381

commit v3 on v2

--- a/solution.py
+++ b/solution.py
@@ -16,7 +16,8 @@
 
 def kernel(
     n,
-    units,
+    policy_hidden,
+    ref_hidden,
     lengths,
     policy_head,
     ref_head,
@@ -96,6 +97,13 @@
         return carry
 
     lax.fori_loop(1, n, greet, 0)
+    for j in range(2):
+        for q in range(2):
+            span = pl.ds(j * half + q * quarter, quarter)
+            both = jnp.concatenate(
+                (policy_hidden[:, span].astype(F32), ref_hidden[:, span].astype(F32)), axis=0
+            )
+            gathered[j, me, 8 * q : 8 * q + 8] = both.astype(BF16)
     pl.semaphore_wait(barrier, n - 1)
 
     sent = []
@@ -129,11 +137,9 @@
         remote(slot, slot, gather_send.at[j, 0, 0], gather_recv.at[j, owner], sibling).wait_recv()
 
     for j in range(2):
-        pass_on(j, units.at[j], me, 0, 0, right)
-        pass_on(j, units.at[j], me, 1, 0, left)
-        pass_on(j, units.at[j], me, 2, 0, sibling)
-    for j in range(2):
-        gathered[j, me] = units[j]
+        pass_on(j, gathered.at[j, me], me, 0, 0, right)
+        pass_on(j, gathered.at[j, me], me, 1, 0, left)
+        pass_on(j, gathered.at[j, me], me, 2, 0, sibling)
     for step in range(1, longer + 1):
         for j in range(2):
             for way in range(2):
@@ -322,6 +328,28 @@
         copy.wait_send()
 
 
+def finish(rows, grad, hidden, kl, head_out, hidden_out, kl_out):
+    head_out[...] = lax.dot_general(
+        rows[...], grad[...], (((0,), (0,)), ((), ())), preferred_element_type=F32
+    ).astype(BF16)
+
+    @pl.when(pl.program_id(0) == 0)
+    def _():
+        tok_dev = kl_out.shape[0]
+        width = hidden.shape[2]
+        for j in range(2):
+            for a in range(4):
+                start = (4 * j + a) * width
+                hidden_out[:, start : start + width] = hidden[
+                    j, a * tok_dev : (a + 1) * tok_dev
+                ]
+        first = lax.axis_index("vocab") * tok_dev
+        padded = kl.shape[1]
+        whole = jnp.broadcast_to(kl[...], (8, padded))
+        turned = pltpu.roll(whole, lax.rem(padded - first, padded), 1)
+        kl_out[...] = turned[0, :tok_dev]
+
+
 def body(policy_hidden, ref_hidden, policy_head, ref_head, lengths):
     n = lax.axis_size("vocab")
     tok_dev, depth = policy_hidden.shape
@@ -331,8 +359,6 @@
     padded = -(-tokens // 128) * 128
     steps = chips // 2 + 1
     quarter, eighth = depth // 4, depth // 8
-    units = jnp.concatenate((policy_hidden, ref_hidden), axis=0)
-    units = units.reshape(8, 2, 2, quarter).transpose(1, 2, 0, 3).reshape(2, 16, quarter)
     vmem = pl.BlockSpec(memory_space=pltpu.VMEM)
     hbm = pl.BlockSpec(memory_space=pl.ANY)
     dma = pltpu.SemaphoreType.DMA
@@ -344,7 +370,7 @@
             jax.ShapeDtypeStruct((tokens, columns), BF16),
             jax.ShapeDtypeStruct((tokens, depth), BF16),
         ),
-        in_specs=[vmem, pl.BlockSpec(memory_space=pltpu.SMEM), hbm, hbm],
+        in_specs=[vmem, vmem, pl.BlockSpec(memory_space=pltpu.SMEM), hbm, hbm],
         out_specs=(vmem,) * 4,
         scratch_shapes=[
             pltpu.VMEM((2, n, 16, quarter), BF16),
@@ -372,15 +398,29 @@
         compiler_params=pltpu.CompilerParams(
             collective_id=0, has_side_effects=True, vmem_limit_bytes=56 * 2**20
         ),
-    )(units, lengths, policy_head, ref_head)
-    own_first = lax.axis_index("vocab") * tok_dev
-    kl_token = lax.dynamic_slice_in_dim(kl[0], own_first, tok_dev)
-    hidden_grad = (
-        hidden.reshape(2, 4, tok_dev, eighth).transpose(2, 0, 1, 3).reshape(tok_dev, depth)
-    )
-    head_grad = lax.dot_general(
-        rows, grad, (((0,), (0,)), ((), ())), preferred_element_type=F32
-    ).astype(BF16)
+    )(policy_hidden, ref_hidden, lengths, policy_head, ref_head)
+    block = 512
+    head_grad, hidden_grad, kl_token = pl.pallas_call(
+        finish,
+        grid=(depth // block,),
+        in_specs=[
+            pl.BlockSpec((tokens, block), lambda i: (0, i)),
+            pl.BlockSpec((tokens, columns), lambda i: (0, 0)),
+            pl.BlockSpec(hidden.shape, lambda i: (0, 0, 0)),
+            pl.BlockSpec((1, padded), lambda i: (0, 0)),
+        ],
+        out_specs=(
+            pl.BlockSpec((block, columns), lambda i: (i, 0)),
+            pl.BlockSpec((tok_dev, depth), lambda i: (0, 0)),
+            pl.BlockSpec((tok_dev,), lambda i: (0,)),
+        ),
+        out_shape=(
+            jax.ShapeDtypeStruct((depth, columns), BF16),
+            jax.ShapeDtypeStruct((tok_dev, depth), F32),
+            jax.ShapeDtypeStruct((tok_dev,), F32),
+        ),
+        compiler_params=pltpu.CompilerParams(vmem_limit_bytes=32 * 2**20),
+    )(rows, grad, hidden, kl)
     return kl_token, hidden_grad, head_grad
 
 

time: 67.3 us -> 66.1 us (0.982)
  matrix products: 9.39 us -> 0 us
  Pallas kernels: 52 us -> 61 us
  other arithmetic: 1.52 us -> 0 us
  local copies, waits for them, and re-layouts: 2.82 us -> 3.5 us
    dot_general x1 -> x0, matrix products: 9.39 us -> none  [body(): lax.dot_general(rows, grad, (((0,), (0,)), ((), ())), preferred_element_t...]
    pallas_call x0 -> x1, Pallas kernels: none -> 9.14 us  [body(): pl.pallas_call(finish, grid=(depth // block,), in_specs=[pl.BlockSpec((to...]
    unnamed x0 -> x8, local copies, waits for them, and re-layouts: none -> 3.5 us
    reshape x1 -> x0, local copies, waits for them, and re-layouts: 1.56 us -> none  [body(): hidden.reshape(2, 4, tok_dev, eighth).transpose(2, 0, 1, 3)]
    concatenate x1 -> x0, other arithmetic: 1.52 us -> none  [body(): units = jnp.concatenate((policy_hidden, ref_hidden), axis=0)]
    dynamic_slice x1 -> x0, local copies, waits for them, and re-layouts: 1.26 us -> none  [body(): kl_token = lax.dynamic_slice_in_dim(kl[0], own_first, tok_dev)]
where the time goes in v3:
time: 66.1 us; the launch traced here: 65.8 us
  Pallas kernels  61 us (92%)
  local copies, waits for them, and re-layouts  3.5 us (5%)
  between operations  1.3 us (2%)
    pallas_call x1, Pallas kernels, body(): pl.pallas_call(functools.partial(kernel, n), out_shape=(jax.ShapeDtypeStr...  51.9 us
    pallas_call x1, Pallas kernels, body(): pl.pallas_call(finish, grid=(depth // block,), in_specs=[pl.BlockSpec((to...  9.14 us
    unnamed x8, local copies, waits for them, and re-layouts  3.5 us

profile of v3, /device:TPU:0, one launch (start us, length us, event | category | flops | bytes accessed | tf_op | source)
XLA Modules:
  0.0 65.8 jit_solution(10140244961527777023)
XLA Ops:
  1.3 51.9 %shard_map.76 = (f32[1,128]{1,0:T(1,128)}, f32[2,16,768]{2,1,0:T(8,128)}, bf16[64,1024]{1,0:T(8,128)(2,1)}, bf16[64,6144]{1,0:T(8,128)(2,1)}) custom-call(bf16[4,6144]{1,0:T(4,128)(2,1)} %policy_hidden.1, bf16[4,6144]{1,0:T(4,128)(2,1)} %ref_hidden.1, s32[1]{0:T(128)S(6)} %copy.8.lengths, bf16[6144,1024]{1,0:T(8,128)(2,1)} %policy_head.1, ...), custom_call_target="tpu_custom_call" | custom-call | tf_op jit(solution)/shard_map/pallas_call | solution.py:365
  53.2 0.0 copy-start
  53.2 1.1 %copy-done = bf16[64,6144]{1,0:T(8,128)(2,1)S(1)} copy-done((bf16[64,6144]{1,0:T(8,128)(2,1)S(1)}, bf16[64,6144]{1,0:T(8,128)(2,1)}, u32[]{:S(2)}) %copy-start) | copy-done | bytes 786456
  54.3 0.0 copy-start.1
  54.3 0.9 %copy-done.1 = bf16[64,1024]{1,0:T(8,128)(2,1)S(1)} copy-done((bf16[64,1024]{1,0:T(8,128)(2,1)S(1)}, bf16[64,1024]{1,0:T(8,128)(2,1)}, u32[]{:S(2)}) %copy-start.1) | copy-done | bytes 131096
  55.2 0.0 copy-start.2
  55.2 0.9 %copy-done.2 = f32[2,16,768]{2,1,0:T(8,128)S(1)} copy-done((f32[2,16,768]{2,1,0:T(8,128)S(1)}, f32[2,16,768]{2,1,0:T(8,128)}, u32[]{:S(2)}) %copy-start.2) | copy-done | bytes 98328
  56.1 0.0 copy-start.3
  56.1 0.6 copy-done.3
  56.7 9.1 %shard_map.77 = (bf16[6144,1024]{1,0:T(8,128)(2,1)}, f32[4,6144]{1,0:T(4,128)}, f32[4]{0:T(128)}) custom-call(bf16[64,6144]{1,0:T(8,128)(2,1)S(1)} %copy-done, bf16[64,1024]{1,0:T(8,128)(2,1)S(1)} %copy-done.1, f32[2,16,768]{2,1,0:T(8,128)S(1)} %copy-done.2, f32[1,128]{1,0:T(1,128)S(1)} %copy-done.3), custom_call_target="tpu_custom_call" | custom-call | tf_op jit(solution)/shard_map/pallas_call | solution.py:403
Async XLA Ops:
  53.2 1.1 %copy-start = (bf16[64,6144]{1,0:T(8,128)(2,1)S(1)}, bf16[64,6144]{1,0:T(8,128)(2,1)}, u32[]{:S(2)}) copy-start(bf16[64,6144]{1,0:T(8,128)(2,1)} %get-tuple-element.10.rows) | copy-start | bytes 2359300
  54.3 0.9 %copy-start.1 = (bf16[64,1024]{1,0:T(8,128)(2,1)S(1)}, bf16[64,1024]{1,0:T(8,128)(2,1)}, u32[]{:S(2)}) copy-start(bf16[64,1024]{1,0:T(8,128)(2,1)} %get-tuple-element.11.grad) | copy-start | bytes 393220
  55.2 0.9 %copy-start.2 = (f32[2,16,768]{2,1,0:T(8,128)S(1)}, f32[2,16,768]{2,1,0:T(8,128)}, u32[]{:S(2)}) copy-start(f32[2,16,768]{2,1,0:T(8,128)} %get-tuple-element.12.hidden) | copy-start | bytes 294916
  56.1 0.6 copy-start.3

commit v4 on v3

--- a/solution.py
+++ b/solution.py
@@ -248,10 +248,9 @@
     grad_out[...] = (weight * jnp.exp(p_logp) * ((p_logp - r_logp) - kl)).astype(BF16)
 
     low = lax.broadcasted_iota(jnp.int32, (chips, 8, TILE), 1) < 4
-    for j in range(2):
-
-        @pl.loop(0, eighth // TILE)
-        def _(i, j=j):
+    def share(j, first, last):
+        @pl.loop(first, last)
+        def _(i):
             cols = pl.ds(pl.multiple_of(i * TILE, TILE), TILE)
             outs = []
             for a in range(4):
@@ -277,6 +276,7 @@
                 total[j, c, :, :, cols] = both
                 outgoing[j, c, :, :, cols] = both.astype(BF16)
 
+    def pair_start(j):
         send(
             outgoing.at[j, 1 - core],
             sibling_in.at[j],
@@ -294,29 +294,41 @@
             slot, slot, ring_send.at[j, way, step], ring_recv.at[j, way, step], sibling
         ).wait_recv()
 
+    def ring_step(j, step):
+        if step == 0:
+            remote(
+                sibling_in.at[j], sibling_in.at[j], pair_send.at[j], pair_recv.at[j], sibling
+            ).wait_recv()
+        for way in range(2):
+            limit = limits[way][j]
+            if step >= limit:
+                continue
+            hops = limit - step
+            value = own(j, chip_at(pos + hops if way == 0 else pos - hops))
+            if step > 0:
+                ring_wait(j, way, step - 1)
+                value = value + ring_in[j, way, step - 1].astype(F32)
+            ring_out[j, way, step] = value.astype(BF16)
+            send(
+                ring_out.at[j, way, step],
+                ring_in.at[j, way, step],
+                ring_send.at[j, way, step],
+                ring_recv.at[j, way, step],
+                (right, left)[way],
+            )
+    tiles = eighth // TILE
+    share(0, 0, tiles)
+    pair_start(0)
+    for i in range(tiles):
+        share(1, i, i + 1)
+        if i == tiles - 1:
+            pair_start(1)
+        if i < longer:
+            ring_step(0, i)
     for step in range(longer):
-        for j in range(2):
-            if step == 0:
-                remote(
-                    sibling_in.at[j], sibling_in.at[j], pair_send.at[j], pair_recv.at[j], sibling
-                ).wait_recv()
-            for way in range(2):
-                limit = limits[way][j]
-                if step >= limit:
-                    continue
-                hops = limit - step
-                value = own(j, chip_at(pos + hops if way == 0 else pos - hops))
-                if step > 0:
-                    ring_wait(j, way, step - 1)
-                    value = value + ring_in[j, way, step - 1].astype(F32)
-                ring_out[j, way, step] = value.astype(BF16)
-                send(
-                    ring_out.at[j, way, step],
-                    ring_in.at[j, way, step],
-                    ring_send.at[j, way, step],
-                    ring_recv.at[j, way, step],
-                    (right, left)[way],
-                )
+        ring_step(1, step)
+        if step + tiles < longer:
+            ring_step(0, step + tiles)
     for j in range(2):
         value = own(j, chip)
         for way in range(2):

time: 66.1 us -> 69.3 us (1.048)
  Pallas kernels: 61 us -> 64.2 us
    pallas_call x1, Pallas kernels: 51.9 us -> 55 us  [body(): pl.pallas_call(functools.partial(kernel, n), out_shape=(jax.ShapeDtypeStr...]
where the time goes in v4:
time: 69.3 us; the launch traced here: 69 us
  Pallas kernels  64.2 us (93%)
  local copies, waits for them, and re-layouts  3.5 us (5%)
  between operations  1.3 us (2%)
    pallas_call x1, Pallas kernels, body(): pl.pallas_call(functools.partial(kernel, n), out_shape=(jax.ShapeDtypeStr...  55 us
    pallas_call x1, Pallas kernels, body(): pl.pallas_call(finish, grid=(depth // block,), in_specs=[pl.BlockSpec((to...  9.14 us
    unnamed x8, local copies, waits for them, and re-layouts  3.5 us

profile of v4, /device:TPU:0, one launch (start us, length us, event | category | flops | bytes accessed | tf_op | source)
XLA Modules:
  0.0 69.0 jit_solution(5500535057141459203)
XLA Ops:
  1.3 55.0 %shard_map.76 = (f32[1,128]{1,0:T(1,128)}, f32[2,16,768]{2,1,0:T(8,128)}, bf16[64,1024]{1,0:T(8,128)(2,1)}, bf16[64,6144]{1,0:T(8,128)(2,1)}) custom-call(bf16[4,6144]{1,0:T(4,128)(2,1)} %policy_hidden.1, bf16[4,6144]{1,0:T(4,128)(2,1)} %ref_hidden.1, s32[1]{0:T(128)S(6)} %copy.8.lengths, bf16[6144,1024]{1,0:T(8,128)(2,1)} %policy_head.1, ...), custom_call_target="tpu_custom_call" | custom-call | tf_op jit(solution)/shard_map/pallas_call | solution.py:377
  56.3 0.0 copy-start
  56.3 1.1 %copy-done = bf16[64,6144]{1,0:T(8,128)(2,1)S(1)} copy-done((bf16[64,6144]{1,0:T(8,128)(2,1)S(1)}, bf16[64,6144]{1,0:T(8,128)(2,1)}, u32[]{:S(2)}) %copy-start) | copy-done | bytes 786456
  57.5 0.0 copy-start.1
  57.5 0.9 %copy-done.1 = bf16[64,1024]{1,0:T(8,128)(2,1)S(1)} copy-done((bf16[64,1024]{1,0:T(8,128)(2,1)S(1)}, bf16[64,1024]{1,0:T(8,128)(2,1)}, u32[]{:S(2)}) %copy-start.1) | copy-done | bytes 131096
  58.4 0.0 copy-start.2
  58.4 0.9 %copy-done.2 = f32[2,16,768]{2,1,0:T(8,128)S(1)} copy-done((f32[2,16,768]{2,1,0:T(8,128)S(1)}, f32[2,16,768]{2,1,0:T(8,128)}, u32[]{:S(2)}) %copy-start.2) | copy-done | bytes 98328
  59.3 0.0 copy-start.3
  59.3 0.6 copy-done.3
  59.8 9.1 %shard_map.77 = (bf16[6144,1024]{1,0:T(8,128)(2,1)}, f32[4,6144]{1,0:T(4,128)}, f32[4]{0:T(128)}) custom-call(bf16[64,6144]{1,0:T(8,128)(2,1)S(1)} %copy-done, bf16[64,1024]{1,0:T(8,128)(2,1)S(1)} %copy-done.1, f32[2,16,768]{2,1,0:T(8,128)S(1)} %copy-done.2, f32[1,128]{1,0:T(1,128)S(1)} %copy-done.3), custom_call_target="tpu_custom_call" | custom-call | tf_op jit(solution)/shard_map/pallas_call | solution.py:415
Async XLA Ops:
  56.3 1.1 %copy-start = (bf16[64,6144]{1,0:T(8,128)(2,1)S(1)}, bf16[64,6144]{1,0:T(8,128)(2,1)}, u32[]{:S(2)}) copy-start(bf16[64,6144]{1,0:T(8,128)(2,1)} %get-tuple-element.10.rows) | copy-start | bytes 2359300
  57.5 0.9 %copy-start.1 = (bf16[64,1024]{1,0:T(8,128)(2,1)S(1)}, bf16[64,1024]{1,0:T(8,128)(2,1)}, u32[]{:S(2)}) copy-start(bf16[64,1024]{1,0:T(8,128)(2,1)} %get-tuple-element.11.grad) | copy-start | bytes 393220
  58.4 0.9 %copy-start.2 = (f32[2,16,768]{2,1,0:T(8,128)S(1)}, f32[2,16,768]{2,1,0:T(8,128)}, u32[]{:S(2)}) copy-start(f32[2,16,768]{2,1,0:T(8,128)} %get-tuple-element.12.hidden) | copy-start | bytes 294916
  59.3 0.6 copy-start.3
